TPU v7x, 32 devices: a whole 2x2x4 slice. The times are simulated.
32 devices in a mesh: blocks: 2 (over y), space: 4 (over z), tm: 2 (over x), span: 2 (over core).
Axes of the slice: x: 2, y: 2, z: 4, core: 2. Of those that a mesh axis runs over, the one named last changes fastest.
Arguments:
- snapshots: float32 [320, 64, 512], P(('blocks', 'tm'), 'space', 'span'), parts along dimension 0, may hold values from -6 to 6
- lagrange_weights: float32 [512, 6], P(('blocks', 'tm')), parts along dimension 0, may hold values from -3 to 3
- source_start: int32 [512], P(('blocks', 'tm')), parts along dimension 0, may hold values from 0 to 156
- band_len: int32 [512], P(('blocks', 'tm')), parts along dimension 0, may hold values from 4 to 6
- band_list: int32 [8], replicated, may hold values from 0 to 15, as said below
- row_metric: float32 [64], P('space'), may hold values from 0.5 to 2
Outputs:
- spectra: float32 [256, 2, 64, 512], P(('blocks', 'space', 'tm'), None, None, 'span'), parts along dimension 0
There are 2 independent parts, one for each index of `blocks`. A program takes and returns all parts, laid end to end along the dimension named above; an argument that names none is the same for every part. Nothing has to cross between parts.
Inputs may be any that keep to these rules, and one draw needn't show every extreme that they name: `band_list`: 8 distinct band numbers.
All inputs are finite; a program needn't handle non-finite values.
Results may differ from a plain program's by a relative error of at most 0.0001.
Values sent between devices are 32-bit elements; how exact they have to be, the bound alone decides.
A program may use at most 64 MiB of HBM per device.

v0:
```python
import math
import jax
import jax.numpy as jnp
from jax import lax
from jax.sharding import PartitionSpec as P

HALO = 16
NT = 256
BW = 8
NL = 8


def extended(cells, sides, width, closed):
    for axis, dim in sides:
        count = lax.axis_size(axis)
        ends = count if closed else count - 1
        head = lax.slice_in_dim(cells, 0, width, axis=dim)
        tail = lax.slice_in_dim(cells, cells.shape[dim] - width, cells.shape[dim], axis=dim)
        cells = jnp.concatenate(
            [
                lax.ppermute(tail, axis, [(i, (i + 1) % count) for i in range(ends)]),
                cells,
                lax.ppermute(head, axis, [((i + 1) % count, i) for i in range(ends)]),
            ],
            axis=dim,
        )
    return cells


def dft_rows(band_list, row_ids, first_sample, count):
    listed_idx = row_ids // 2
    is_imag = row_ids % 2
    band_pos = listed_idx // BW
    matches = band_pos[:, None] == jnp.arange(band_list.shape[0])[None, :]
    band_of = jnp.sum(jnp.where(matches, band_list[None, :], 0), axis=1)
    frequency = band_of * BW + listed_idx % BW
    sample_ids = first_sample + jnp.arange(count)
    phase_idx = frequency[:, None] * sample_ids[None, :] % NT
    angles = 2.0 * math.pi / NT * phase_idx.astype(jnp.float32)
    window = 0.5 - 0.5 * jnp.cos(2.0 * math.pi / NT * sample_ids.astype(jnp.float32))
    weighting = window / math.sqrt(NT)
    waves = jnp.where(is_imag[:, None] == 0, jnp.cos(angles), -jnp.sin(angles))
    return waves * weighting[None, :]


def shards(snapshots, lagrange_weights, source_start, band_len, band_list, row_metric):
    tm_index = lax.axis_index("tm")
    n_tm, n_space = (lax.axis_size("tm"), lax.axis_size("space"))
    steps_dev, rows_dev, span_cells = snapshots.shape
    samples = source_start.shape[0]
    reach = extended(snapshots, (("tm", 0),), HALO, False)
    reach_len = steps_dev + 2 * HALO
    anchor = tm_index * steps_dev - HALO
    slot_ids = jnp.arange(6)
    columns = source_start[:, None] + slot_ids[None, :] - anchor
    active = slot_ids[None, :] < band_len[:, None]
    selected = (columns[:, :, None] == jnp.arange(reach_len)[None, None, :]) & active[:, :, None]
    interp_matrix = jnp.sum(
        jnp.where(selected, lagrange_weights[:, :, None], jnp.float32(0.0)), axis=1
    )
    total_rows = 2 * NL * BW
    own = total_rows // (n_tm * n_space)
    positions = jnp.arange(total_rows).reshape(n_space, n_tm, own).transpose(1, 0, 2).reshape(-1)
    coeffs = dft_rows(band_list, positions, tm_index * samples, samples)
    combined = jnp.dot(coeffs, interp_matrix, precision=lax.Precision.HIGHEST)
    partial = jnp.dot(
        combined, reach.reshape(reach_len, rows_dev * span_cells), precision=lax.Precision.HIGHEST
    )
    summed = lax.psum_scatter(partial, "tm", scatter_dimension=0, tiled=True)
    summed = summed.reshape(n_space * own, rows_dev, span_cells)
    fields = lax.all_to_all(summed, "space", split_axis=0, concat_axis=1, tiled=True)
    metric = lax.all_gather(row_metric, "space", tiled=True)
    row_padded = jnp.pad(fields, ((0, 0), (1, 1), (0, 0)))
    along_rows = 0.5 * metric[None, :, None] * (row_padded[:, 2:, :] - row_padded[:, :-2, :])
    span_padded = extended(fields, (("span", 2),), 1, True)
    along_span = 0.5 * (span_padded[:, :, 2:] - span_padded[:, :, :-2])
    return jnp.stack((along_rows, along_span), axis=1)


def solution(mesh):
    placed = (
        P(("blocks", "tm"), "space", "span"),
        P(("blocks", "tm"), None),
        P(("blocks", "tm")),
        P(("blocks", "tm")),
        P(),
        P("space"),
    )
    return jax.shard_map(
        shards,
        mesh=mesh,
        in_specs=placed,
        out_specs=P(("blocks", "space", "tm"), None, None, "span"),
        check_vma=False,
    )
```

profile of v0, /device:TPU:0, one launch (start us, length us, event | category | flops | bytes accessed | tf_op | source)
XLA Modules:
  0.0 104.5 jit_solution(15764756894311047526)
XLA Ops:
  6.5 1.2 %fusion.34 = (f32[16,16,256]{2,1,0:T(8,128)S(1)}, f32[16,16,256]{2,1,0:T(8,128)S(1)}) fusion(f32[80,16,256]{2,1,0:T(8,128)} %param.6), kind=kLoop, calls=%fused_computation.64 | loop fusion | bytes 1048576 | tf_op jit(solution)/shard_map/slice | solution.py:18
  7.7 4.9 %collective-permute-start = (f32[16,16,256]{2,1,0:T(8,128)S(1)}, f32[16,16,256]{2,1,0:T(8,128)S(1)}, u32[]{:S(2)}, u32[]{:S(2)}) collective-permute-start(f32[16,16,256]{2,1,0:T(8,128)S(1)} %get-tuple-element.7), channel_id=1, source_target_pairs={{0,2},{1,3},{4,6},{5,7},{8,10},{9,11},{12,14},{13,15},{16,18},{17,... | collective-permute-start | bytes 786440 | tf_op jit(solution)/shard_map/ppermute | solution.py:21
  12.6 1.3 %collective-permute-start.1 = (f32[16,16,256]{2,1,0:T(8,128)S(1)}, f32[16,16,256]{2,1,0:T(8,128)S(1)}, u32[]{:S(2)}, u32[]{:S(2)}) collective-permute-start(f32[16,16,256]{2,1,0:T(8,128)S(1)} %get-tuple-element.8), channel_id=1, source_target_pairs={{2,0},{3,1},{6,4},{7,5},{10,8},{11,9},{14,12},{15,13},{18,16},{19,... | collective-permute-start | bytes 786440 | tf_op jit(solution)/shard_map/ppermute | solution.py:23
  13.9 0.1 reshape.208
  14.0 0.7 iota_compare_fusion.1
  14.7 0.7 add_subtract_fusion
  15.3 0.7 select_reduce_fusion.1
  16.1 0.8 select_reduce_fusion
  16.9 0.1 subtract_multiply_fusion
  16.9 0.5 fusion.10
  17.5 0.6 collective-permute-done
  18.1 4.1 %collective-permute-done.1 = f32[16,16,256]{2,1,0:T(8,128)S(1)} collective-permute-done((f32[16,16,256]{2,1,0:T(8,128)S(1)}, f32[16,16,256]{2,1,0:T(8,128)S(1)}, u32[]{:S(2)}, u32[]{:S(2)}) %collective-permute-start.1) | collective-permute-done | bytes 262176 | tf_op jit(solution)/shard_map/ppermute | solution.py:23
  22.2 0.1 pad_maximum_fusion.1
  22.4 1.4 %copy.12 = f32[14,8,16,256]{3,1,2,0:T(8,128)S(1)} copy(f32[14,8,16,256]{3,2,1,0:T(8,128)S(1)} %bitcast.20) | data formatting | bytes 3670016
  23.8 3.2 %fusion.36 = f32[128,4096]{1,0:T(8,128)} fusion(f32[128,112]{1,0:T(8,128)S(1)} %fusion.10, f32[112,4096]{1,0:T(8,128)S(1)} %bitcast.21), kind=kOutput, calls=%fused_computation.66 | convolution fusion | flops 704643072 | bytes 3989504 | tf_op jit(solution)/shard_map/dot_general | solution.py:66
  26.9 0.0 reduce-scatter.2.cloned.1.call-update
  27.0 32.3 %reduce-scatter.2.cloned.1.call-done = f32[64,4096]{1,0:T(8,128)} async-done(((f32[128,4096]{1,0:T(8,128)}), f32[64,4096]{1,0:T(8,128)}) %reduce-scatter.2.cloned.1.call-update) | async-done | bytes 1048592 | tf_op jit(solution)/shard_map/reduce_scatter | solution.py:69
  59.3 2.5 %copy.13 = f32[8,8,16,256]{3,2,1,0:T(8,128)} copy(f32[8,8,16,256]{3,1,2,0:T(8,128)} %bitcast.23) | data formatting | bytes 2097152
  61.8 4.6 %all-to-all-start = ((f32[64,16,256]{2,1,0:T(8,128)}), f32[64,16,256]{2,1,0:T(8,128)S(1)}, u32[]{:S(2)}, u32[]{:S(2)}) async-start(f32[64,16,256]{2,1,0:T(8,128)} %bitcast.12), calls=%async_computation.1 | async-start | bytes 2097152 | tf_op jit(solution)/shard_map/all_to_all | solution.py:71
  66.4 0.0 copy-done.2
  66.4 0.6 dynamic-slice
  67.6 0.2 dynamic-update-slice
  67.8 21.8 %all-reduce.1 = f32[64]{0:T(128)S(1)} all-reduce(f32[64]{0:T(128)S(1)} %dynamic-update-slice), channel_id=1, replica_groups=mesh['blocks'=2,'space'=4,'tm'=2,'span'=2] {'space'}, use_global_device_ids=true, to_apply=%add.1 | all-reduce | flops 64 | bytes 512
  89.6 2.7 %all-to-all-done = f32[64,16,256]{2,1,0:T(8,128)S(1)} async-done(((f32[64,16,256]{2,1,0:T(8,128)}), f32[64,16,256]{2,1,0:T(8,128)S(1)}, u32[]{:S(2)}, u32[]{:S(2)}) %all-to-all-start) | async-done | bytes 1048608 | tf_op jit(solution)/shard_map/all_to_all | solution.py:71
  92.3 0.1 copy.10
  92.4 0.2 fusion.35
  92.6 0.1 collective-permute-start.2
  92.7 0.5 collective-permute-start.3
  93.2 1.4 %collective-permute-done.2 = f32[16,64,1]{2,1,0:T(8,128)S(1)} collective-permute-done((f32[16,64,1]{2,1,0:T(8,128)S(1)}, f32[16,64,1]{2,1,0:T(8,128)S(1)}, u32[]{:S(2)}, u32[]{:S(2)}) %collective-permute-start.2) | collective-permute-done | bytes 4128 | tf_op jit(solution)/shard_map/ppermute | solution.py:23
  94.6 0.7 collective-permute-done.3
  95.4 0.8 fusion.2
  96.2 1.5 %pad_maximum_fusion = f32[16,2,64,256]{3,2,1,0:T(8,128)} fusion(f32[16,1,64,256]{3,2,1,0:T(8,128)S(1)} %get-tuple-element.10, f32[16,1,64,256]{3,2,1,0:T(8,128)S(1)} %get-tuple-element.9), kind=kLoop, calls=%fused_computation | loop fusion | flops 524288 | bytes 4194304 | tf_op jit(solution)/shard_map/stack | solution.py:77
  (12 shorter events, 0.1 us)
Async XLA Ops:
  6.5 15.7 %copy-start = (f32[80,16,256]{2,1,0:T(8,128)S(1)}, f32[80,16,256]{2,1,0:T(8,128)}, u32[]{:S(2)}) copy-start(f32[80,16,256]{2,1,0:T(8,128)} %param.6) | copy-start | bytes 3932164
  6.5 52.7 %reduce-scatter.2.cloned.1.call-start = ((), (), s32[]{:S(2)}) async-start(), calls=%async_computation.2 | async-start | bytes 3145728 | tf_op jit(solution)/shard_map/reduce_scatter | solution.py:69
  7.7 10.4 %collective-permute-start = (f32[16,16,256]{2,1,0:T(8,128)S(1)}, f32[16,16,256]{2,1,0:T(8,128)S(1)}, u32[]{:S(2)}, u32[]{:S(2)}) collective-permute-start(f32[16,16,256]{2,1,0:T(8,128)S(1)} %get-tuple-element.7), channel_id=1, source_target_pairs={{0,2},{1,3},{4,6},{5,7},{8,10},{9,11},{12,14},{13,15},{16,18},{17,... | collective-permute-start | bytes 786440 | tf_op jit(solution)/shard_map/ppermute | solution.py:21
  12.6 9.7 %collective-permute-start.1 = (f32[16,16,256]{2,1,0:T(8,128)S(1)}, f32[16,16,256]{2,1,0:T(8,128)S(1)}, u32[]{:S(2)}, u32[]{:S(2)}) collective-permute-start(f32[16,16,256]{2,1,0:T(8,128)S(1)} %get-tuple-element.8), channel_id=1, source_target_pairs={{2,0},{3,1},{6,4},{7,5},{10,8},{11,9},{14,12},{15,13},{18,16},{19,... | collective-permute-start | bytes 786440 | tf_op jit(solution)/shard_map/ppermute | solution.py:23
  59.3 7.1 %copy-start.2 = (u32[32]{0:T(128)S(1)}, u32[32]{0:T(128)}, u32[]{:S(2)}) copy-start(u32[32]{0:T(128)} %constant.95) | copy-start | bytes 388
  59.3 8.3 %copy-start.1 = (f32[16]{0:T(128)S(1)}, f32[16]{0:T(128)}, u32[]{:S(2)}) copy-start(f32[16]{0:T(128)} %param.11) | copy-start | bytes 196
  61.8 30.5 %all-to-all-start = ((f32[64,16,256]{2,1,0:T(8,128)}), f32[64,16,256]{2,1,0:T(8,128)S(1)}, u32[]{:S(2)}, u32[]{:S(2)}) async-start(f32[64,16,256]{2,1,0:T(8,128)} %bitcast.12), calls=%async_computation.1 | async-start | bytes 2097152 | tf_op jit(solution)/shard_map/all_to_all | solution.py:71
  92.6 2.0 %collective-permute-start.2 = (f32[16,64,1]{2,1,0:T(8,128)S(1)}, f32[16,64,1]{2,1,0:T(8,128)S(1)}, u32[]{:S(2)}, u32[]{:S(2)}) collective-permute-start(f32[16,64,1]{2,1,0:T(8,128)S(1)} %get-tuple-element.11), channel_id=1, source_target_pairs={{1,0},{0,1},{3,2},{2,3},{5,4},{4,5},{7,6},{6,7},{9,8},{8,9},{11,10... | collective-permute-start | bytes 12296 | tf_op jit(solution)/shard_map/ppermute | solution.py:23
  92.7 2.6 %collective-permute-start.3 = (f32[16,64,1]{2,1,0:T(8,128)S(1)}, f32[16,64,1]{2,1,0:T(8,128)S(1)}, u32[]{:S(2)}, u32[]{:S(2)}) collective-permute-start(f32[16,64,1]{2,1,0:T(8,128)S(1)} %get-tuple-element.12), channel_id=1, source_target_pairs={{0,1},{1,0},{2,3},{3,2},{4,5},{5,4},{6,7},{7,6},{8,9},{9,8},{10,11... | collective-permute-start | bytes 12296 | tf_op jit(solution)/shard_map/ppermute | solution.py:21
Sparse Core Ops, SparseCore 0:
  27.1 32.1 reduce-scatter.1
where the time goes:
time: 105 us
  waiting for transfers between devices  42 us (40%)
  blocking collectives  21.8 us (21%)
  between operations  14.1 us (13%)
  starting transfers between devices  11.3 us (11%)
  local copies, waits for them, and re-layouts  6.28 us (6%)
  other arithmetic  5.39 us (5%)
  matrix products  3.72 us (4%)
    reduce_scatter x1, waiting for transfers between devices, shards(): summed = lax.psum_scatter(partial, 'tm', scatter_dimension=0, tiled=True)  32.3 us
    unnamed x1, blocking collectives  21.8 us
    ppermute x2, waiting for transfers between devices, extended(): lax.ppermute(head, axis, [((i + 1) % count, i) for i in range(ends)])  5.52 us
    ppermute x2, starting transfers between devices, extended(): lax.ppermute(tail, axis, [(i, (i + 1) % count) for i in range(ends)])  5.36 us
    unnamed x11, local copies, waits for them, and re-layouts  4.74 us
    all_to_all x1, starting transfers between devices, shards(): lax.all_to_all(summed, 'space', split_axis=0, concat_axis=1, tiled=True)  4.59 us
    dot_general x1, matrix products, shards(): jnp.dot(combined, reach.reshape(reach_len, rows_dev * span_cells), precis...  3.18 us
    all_to_all x1, waiting for transfers between devices, shards(): lax.all_to_all(summed, 'space', split_axis=0, concat_axis=1, tiled=True)  2.73 us
  transfers between devices with their start and end apart: 6, of which 6 were waited for; matrix products, arithmetic and copies ran while one was open for 4% of the time, Pallas kernels for 0%

commit v1 on v0

--- a/solution.py
+++ b/solution.py
@@ -8,6 +8,22 @@
 NT = 256
 BW = 8
 NL = 8
+
+
+def pairwise_exchange(array, axis, split, join):
+    ways, here = (lax.axis_size(axis), lax.axis_index(axis))
+    width = array.shape[split] // ways
+    shape = list(array.shape)
+    shape[split] = width
+    height = shape[join]
+    shape[join] = height * ways
+    full = jnp.zeros(shape, array.dtype)
+    for mask in range(ways):
+        part = lax.dynamic_slice_in_dim(array, (here ^ mask) * width, width, axis=split)
+        if mask:
+            part = lax.ppermute(part, axis, [(d, d ^ mask) for d in range(ways)])
+        full = lax.dynamic_update_slice_in_dim(full, part, (here ^ mask) * height, axis=join)
+    return full
 
 
 def extended(cells, sides, width, closed):
@@ -68,7 +84,7 @@
     )
     summed = lax.psum_scatter(partial, "tm", scatter_dimension=0, tiled=True)
     summed = summed.reshape(n_space * own, rows_dev, span_cells)
-    fields = lax.all_to_all(summed, "space", split_axis=0, concat_axis=1, tiled=True)
+    fields = pairwise_exchange(summed, "space", 0, 1)
     metric = lax.all_gather(row_metric, "space", tiled=True)
     row_padded = jnp.pad(fields, ((0, 0), (1, 1), (0, 0)))
     along_rows = 0.5 * metric[None, :, None] * (row_padded[:, 2:, :] - row_padded[:, :-2, :])

time: 105 us -> 101 us (0.962)
  the two profiles are of different devices: /device:TPU:0 before, /device:TPU:17 now
where the time goes in v1:
time: 101 us
  waiting for transfers between devices  39.4 us (39%)
  blocking collectives  22.5 us (22%)
  between operations  14.2 us (14%)
  starting transfers between devices  9.88 us (10%)
  local copies, waits for them, and re-layouts  5.47 us (5%)
  other arithmetic  5.39 us (5%)
  matrix products  3.72 us (4%)
    reduce_scatter x1, waiting for transfers between devices, shards(): summed = lax.psum_scatter(partial, 'tm', scatter_dimension=0, tiled=True)  33.3 us
    unnamed x1, blocking collectives  22.5 us
    ppermute x2, waiting for transfers between devices, extended(): lax.ppermute(head, axis, [((i + 1) % count, i) for i in range(ends)])  5.26 us
    ppermute x2, starting transfers between devices, extended(): lax.ppermute(head, axis, [((i + 1) % count, i) for i in range(ends)])  3.96 us
    unnamed x11, local copies, waits for them, and re-layouts  3.75 us
    ppermute x2, starting transfers between devices, extended(): lax.ppermute(tail, axis, [(i, (i + 1) % count) for i in range(ends)])  3.21 us
    dot_general x1, matrix products, shards(): jnp.dot(combined, reach.reshape(reach_len, rows_dev * span_cells), precis...  3.18 us
    ppermute x3, starting transfers between devices, pairwise_exchange(): part = lax.ppermute(part, axis, [(d, d ^ mask) for d in range(ways)])  2.71 us
  transfers between devices with their start and end apart: 8, of which 5 were waited for; matrix products, arithmetic and copies ran while one was open for 4% of the time, Pallas kernels for 0%

profile of v1, /device:TPU:17, one launch (start us, length us, event | category | flops | bytes accessed | tf_op | source)
XLA Modules:
  0.0 100.5 jit_solution(18077622467783512832)
XLA Ops:
  6.5 1.2 %fusion.34 = (f32[16,16,256]{2,1,0:T(8,128)S(1)}, f32[16,16,256]{2,1,0:T(8,128)S(1)}) fusion(f32[80,16,256]{2,1,0:T(8,128)} %param.6), kind=kLoop, calls=%fused_computation.71 | loop fusion | bytes 1048576 | tf_op jit(solution)/shard_map/slice | solution.py:34
  7.7 3.1 %collective-permute-start = (f32[16,16,256]{2,1,0:T(8,128)S(1)}, f32[16,16,256]{2,1,0:T(8,128)S(1)}, u32[]{:S(2)}, u32[]{:S(2)}) collective-permute-start(f32[16,16,256]{2,1,0:T(8,128)S(1)} %get-tuple-element.7), channel_id=1, source_target_pairs={{0,2},{1,3},{4,6},{5,7},{8,10},{9,11},{12,14},{13,15},{16,18},{17,... | collective-permute-start | bytes 786440 | tf_op jit(solution)/shard_map/ppermute | solution.py:37
  10.8 1.3 %collective-permute-start.1 = (f32[16,16,256]{2,1,0:T(8,128)S(1)}, f32[16,16,256]{2,1,0:T(8,128)S(1)}, u32[]{:S(2)}, u32[]{:S(2)}) collective-permute-start(f32[16,16,256]{2,1,0:T(8,128)S(1)} %get-tuple-element.8), channel_id=1, source_target_pairs={{2,0},{3,1},{6,4},{7,5},{10,8},{11,9},{14,12},{15,13},{18,16},{19,... | collective-permute-start | bytes 786440 | tf_op jit(solution)/shard_map/ppermute | solution.py:39
  12.2 0.1 reshape.208
  12.3 0.7 iota_compare_fusion.1
  13.0 0.7 select_reduce_fusion.1
  13.7 0.7 add_subtract_fusion
  14.4 0.8 select_reduce_fusion
  15.1 0.1 subtract_multiply_fusion
  15.2 0.5 fusion.10
  15.7 0.1 collective-permute-done
  15.8 3.8 %collective-permute-done.1 = f32[16,16,256]{2,1,0:T(8,128)S(1)} collective-permute-done((f32[16,16,256]{2,1,0:T(8,128)S(1)}, f32[16,16,256]{2,1,0:T(8,128)S(1)}, u32[]{:S(2)}, u32[]{:S(2)}) %collective-permute-start.1) | collective-permute-done | bytes 262176 | tf_op jit(solution)/shard_map/ppermute | solution.py:39
  19.6 0.1 pad_maximum_fusion.1
  19.8 1.4 %copy.10 = f32[14,8,16,256]{3,1,2,0:T(8,128)S(1)} copy(f32[14,8,16,256]{3,2,1,0:T(8,128)S(1)} %bitcast.14) | data formatting | bytes 3670016
  21.1 3.2 %fusion.36 = f32[128,4096]{1,0:T(8,128)} fusion(f32[128,112]{1,0:T(8,128)S(1)} %fusion.10, f32[112,4096]{1,0:T(8,128)S(1)} %bitcast.15), kind=kOutput, calls=%fused_computation.73 | convolution fusion | flops 704643072 | bytes 3989504 | tf_op jit(solution)/shard_map/dot_general | solution.py:82
  24.4 33.3 %reduce-scatter.2.cloned.1.call-done = f32[64,4096]{1,0:T(8,128)} async-done(((f32[128,4096]{1,0:T(8,128)}), f32[64,4096]{1,0:T(8,128)}) %reduce-scatter.2.cloned.1.call-update) | async-done | bytes 1048592 | tf_op jit(solution)/shard_map/reduce_scatter | solution.py:85
  57.7 1.5 %copy.11 = f32[8,8,16,256]{3,2,1,0:T(8,128)S(1)} copy(f32[8,8,16,256]{3,1,2,0:T(8,128)} %bitcast.17) | data formatting | bytes 2097152
  59.2 0.1 broadcast_in_dim.31
  59.3 0.1 constant_dynamic-slice_fusion.2
  59.4 1.2 %collective-permute-start.2 = (f32[16,16,256]{2,1,0:T(8,128)S(1)}, f32[16,16,256]{2,1,0:T(8,128)S(1)}, u32[]{:S(2)}, u32[]{:S(2)}) collective-permute-start(f32[16,16,256]{2,1,0:T(8,128)S(1)} %get-tuple-element.15), channel_id=1, source_target_pairs={{0,4},{4,0},{8,12},{12,8},{1,5},{5,1},{9,13},{13,9},{2,6},{6,2},{1... | collective-permute-start | bytes 786440 | tf_op jit(solution)/shard_map/ppermute | solution.py:24
  60.7 0.3 collective-permute-start.3
  60.9 1.2 %collective-permute-start.4 = (f32[16,16,256]{2,1,0:T(8,128)S(1)}, f32[16,16,256]{2,1,0:T(8,128)S(1)}, u32[]{:S(2)}, u32[]{:S(2)}) collective-permute-start(f32[16,16,256]{2,1,0:T(8,128)S(1)} %get-tuple-element.13), channel_id=1, source_target_pairs={{0,12},{4,8},{8,4},{12,0},{1,13},{5,9},{9,5},{13,1},{2,14},{6,10},... | collective-permute-start | bytes 786440 | tf_op jit(solution)/shard_map/ppermute | solution.py:24
  62.1 0.6 dynamic-slice
  63.4 0.2 dynamic-update-slice
  63.6 22.5 %all-reduce.1 = f32[64]{0:T(128)S(1)} all-reduce(f32[64]{0:T(128)S(1)} %dynamic-update-slice), channel_id=1, replica_groups=mesh['blocks'=2,'space'=4,'tm'=2,'span'=2] {'space'}, use_global_device_ids=true, to_apply=%add.1 | all-reduce | flops 64 | bytes 512
  86.2 0.2 fusion.35
  86.4 2.7 %collective-permute-start.5 = (f32[16,64,1]{2,1,0:T(8,128)S(1)}, f32[16,64,1]{2,1,0:T(8,128)S(1)}, u32[]{:S(2)}, u32[]{:S(2)}) collective-permute-start(f32[16,64,1]{2,1,0:T(8,128)S(1)} %get-tuple-element.11), channel_id=1, source_target_pairs={{1,0},{0,1},{3,2},{2,3},{5,4},{4,5},{7,6},{6,7},{9,8},{8,9},{11,10... | collective-permute-start | bytes 12296 | tf_op jit(solution)/shard_map/ppermute | solution.py:39
  89.1 0.1 collective-permute-start.6
  89.2 1.5 %collective-permute-done.5 = f32[16,64,1]{2,1,0:T(8,128)S(1)} collective-permute-done((f32[16,64,1]{2,1,0:T(8,128)S(1)}, f32[16,64,1]{2,1,0:T(8,128)S(1)}, u32[]{:S(2)}, u32[]{:S(2)}) %collective-permute-start.5) | collective-permute-done | bytes 4128 | tf_op jit(solution)/shard_map/ppermute | solution.py:39
  90.6 0.7 collective-permute-done.6
  91.4 0.8 fusion.2
  92.2 1.5 %pad_maximum_fusion = f32[16,2,64,256]{3,2,1,0:T(8,128)} fusion(f32[16,1,64,256]{3,2,1,0:T(8,128)S(1)} %get-tuple-element.10, f32[16,1,64,256]{3,2,1,0:T(8,128)S(1)} %get-tuple-element.9), kind=kLoop, calls=%fused_computation | loop fusion | flops 524288 | bytes 4194304 | tf_op jit(solution)/shard_map/stack | solution.py:93
  (20 shorter events, 0.2 us)
Async XLA Ops:
  6.5 13.1 %copy-start = (f32[80,16,256]{2,1,0:T(8,128)S(1)}, f32[80,16,256]{2,1,0:T(8,128)}, u32[]{:S(2)}) copy-start(f32[80,16,256]{2,1,0:T(8,128)} %param.6) | copy-start | bytes 3932164
  6.5 51.1 %reduce-scatter.2.cloned.1.call-start = ((), (), s32[]{:S(2)}) async-start(), calls=%async_computation.1 | async-start | bytes 3145728 | tf_op jit(solution)/shard_map/reduce_scatter | solution.py:85
  7.7 8.1 %collective-permute-start = (f32[16,16,256]{2,1,0:T(8,128)S(1)}, f32[16,16,256]{2,1,0:T(8,128)S(1)}, u32[]{:S(2)}, u32[]{:S(2)}) collective-permute-start(f32[16,16,256]{2,1,0:T(8,128)S(1)} %get-tuple-element.7), channel_id=1, source_target_pairs={{0,2},{1,3},{4,6},{5,7},{8,10},{9,11},{12,14},{13,15},{16,18},{17,... | collective-permute-start | bytes 786440 | tf_op jit(solution)/shard_map/ppermute | solution.py:37
  10.8 8.8 %collective-permute-start.1 = (f32[16,16,256]{2,1,0:T(8,128)S(1)}, f32[16,16,256]{2,1,0:T(8,128)S(1)}, u32[]{:S(2)}, u32[]{:S(2)}) collective-permute-start(f32[16,16,256]{2,1,0:T(8,128)S(1)} %get-tuple-element.8), channel_id=1, source_target_pairs={{2,0},{3,1},{6,4},{7,5},{10,8},{11,9},{14,12},{15,13},{18,16},{19,... | collective-permute-start | bytes 786440 | tf_op jit(solution)/shard_map/ppermute | solution.py:39
  59.2 3.0 %copy-start.2 = (u32[32]{0:T(128)S(1)}, u32[32]{0:T(128)}, u32[]{:S(2)}) copy-start(u32[32]{0:T(128)} %constant.105) | copy-start | bytes 388
  59.2 4.2 %copy-start.1 = (f32[16]{0:T(128)S(1)}, f32[16]{0:T(128)}, u32[]{:S(2)}) copy-start(f32[16]{0:T(128)} %param.11) | copy-start | bytes 196
  59.4 26.7 %collective-permute-start.2 = (f32[16,16,256]{2,1,0:T(8,128)S(1)}, f32[16,16,256]{2,1,0:T(8,128)S(1)}, u32[]{:S(2)}, u32[]{:S(2)}) collective-permute-start(f32[16,16,256]{2,1,0:T(8,128)S(1)} %get-tuple-element.15), channel_id=1, source_target_pairs={{0,4},{4,0},{8,12},{12,8},{1,5},{5,1},{9,13},{13,9},{2,6},{6,2},{1... | collective-permute-start | bytes 786440 | tf_op jit(solution)/shard_map/ppermute | solution.py:24
  60.7 25.5 %collective-permute-start.3 = (f32[16,16,256]{2,1,0:T(8,128)S(1)}, f32[16,16,256]{2,1,0:T(8,128)S(1)}, u32[]{:S(2)}, u32[]{:S(2)}) collective-permute-start(f32[16,16,256]{2,1,0:T(8,128)S(1)} %get-tuple-element.14), channel_id=1, source_target_pairs={{0,8},{4,12},{8,0},{12,4},{1,9},{5,13},{9,1},{13,5},{2,10},{6,14},... | collective-permute-start | bytes 786440 | tf_op jit(solution)/shard_map/ppermute | solution.py:24
  60.9 25.2 %collective-permute-start.4 = (f32[16,16,256]{2,1,0:T(8,128)S(1)}, f32[16,16,256]{2,1,0:T(8,128)S(1)}, u32[]{:S(2)}, u32[]{:S(2)}) collective-permute-start(f32[16,16,256]{2,1,0:T(8,128)S(1)} %get-tuple-element.13), channel_id=1, source_target_pairs={{0,12},{4,8},{8,4},{12,0},{1,13},{5,9},{9,5},{13,1},{2,14},{6,10},... | collective-permute-start | bytes 786440 | tf_op jit(solution)/shard_map/ppermute | solution.py:24
  86.4 4.2 %collective-permute-start.5 = (f32[16,64,1]{2,1,0:T(8,128)S(1)}, f32[16,64,1]{2,1,0:T(8,128)S(1)}, u32[]{:S(2)}, u32[]{:S(2)}) collective-permute-start(f32[16,64,1]{2,1,0:T(8,128)S(1)} %get-tuple-element.11), channel_id=1, source_target_pairs={{1,0},{0,1},{3,2},{2,3},{5,4},{4,5},{7,6},{6,7},{9,8},{8,9},{11,10... | collective-permute-start | bytes 12296 | tf_op jit(solution)/shard_map/ppermute | solution.py:39
  89.1 2.3 %collective-permute-start.6 = (f32[16,64,1]{2,1,0:T(8,128)S(1)}, f32[16,64,1]{2,1,0:T(8,128)S(1)}, u32[]{:S(2)}, u32[]{:S(2)}) collective-permute-start(f32[16,64,1]{2,1,0:T(8,128)S(1)} %get-tuple-element.12), channel_id=1, source_target_pairs={{0,1},{1,0},{2,3},{3,2},{4,5},{5,4},{6,7},{7,6},{8,9},{9,8},{10,11... | collective-permute-start | bytes 12296 | tf_op jit(solution)/shard_map/ppermute | solution.py:37
Sparse Core Ops, SparseCore 0:
  24.5 33.1 reduce-scatter.1
